TPU v7x, 32 devices: a whole 2x2x4 slice. The times are simulated.
32 devices in a mesh: src: 8 (over z, x), att: 4 (over y, core).
Axes of the slice: x: 2, y: 2, z: 4, core: 2. Of those that a mesh axis runs over, the one named last changes fastest.
Arguments:
- residual: float32 [262144], P(('src', 'att')), may hold values from -6 to 6
- weight: float32 [262144], P(('src', 'att')), may hold values from 0.2 to 5
- source_part: float32 [5, 262144], P(None, ('src', 'att')), may hold values from -6 to 6
- attitude_part: float32 [4, 262144], P(None, ('src', 'att')), may hold values from -6 to 6
- calib_part: float32 [262144], P(('src', 'att')), may hold values from -6 to 6
- phase: float32 [262144], P(('src', 'att')), may hold values from 0 to 1
- obs_source: int32 [262144], P(('src', 'att')), may hold values from 0 to 63
- obs_owner: int32 [262144], P(('src', 'att')), may hold values from 0 to 31
- obs_slot: int32 [262144], P(('src', 'att')), may hold values from 0 to 3
- obs_knot: int32 [262144], P(('src', 'att')), may hold values from 0 to 124
- obs_calib: int32 [262144], P(('src', 'att')), may hold values from 0 to 2047
- tile_count: int32 [32, 4], P(('src', 'att')), may hold values from 1 to 2048, 5120 in all within a row
- time_list: int32 [32, 32, 4], P(None, ('src', 'att')), may hold values from 0 to 7
Outputs:
- source_update: float32 [5, 8192], P(None, ('src', 'att'))
- attitude_update: float32 [4, 32768], P(None, ('src', 'att'))
- calib_update: float32 [2048], replicated
- residual_out: float32 [262144], P(('src', 'att'))
Inputs may be any that keep to these rules, and one draw needn't show every extreme that they name: `tile_count`: each device's tile counts sum to 5120. `time_list`: local knot block of the owner; entries may repeat.
All inputs are finite; a program needn't handle non-finite values.
Results may differ from a plain program's by a relative error of at most 0.0001.
Values sent between devices are 32-bit elements; how exact they have to be, the bound alone decides.
A program may use at most 64 MiB of HBM per device.

v0:
```python
import math
import jax
import jax.numpy as jnp
from jax import lax
from jax.sharding import PartitionSpec as P

OBS_TILE = 2048
SRC_TILE = 64
KNOT = 128
LIST = 4
KB_DEV = 8
NCAL = 2048
HIGH = lax.Precision.HIGHEST


def spline_weights(phase):
    other = 1.0 - phase
    square = phase * phase
    cube = square * phase
    return [
        other * other * other / 6.0,
        (3.0 * cube - 6.0 * square + 4.0) / 6.0,
        (-3.0 * cube + 3.0 * square + 3.0 * phase + 1.0) / 6.0,
        cube / 6.0,
    ]


def solve_normals(sums):
    matrix = [[None] * 5 for _ in range(5)]
    column = 0
    for left in range(5):
        for right in range(left, 5):
            matrix[left][right] = sums[:, column]
            matrix[right][left] = sums[:, column]
            column += 1
    target = [sums[:, 15 + left] for left in range(5)]
    for left in range(5):
        matrix[left][left] = matrix[left][left] + 1.0
    for pivot in range(5):
        for lower in range(pivot + 1, 5):
            factor = matrix[lower][pivot] / matrix[pivot][pivot]
            for right in range(pivot, 5):
                matrix[lower][right] = matrix[lower][right] - factor * matrix[pivot][right]
            target[lower] = target[lower] - factor * target[pivot]
    result = [None] * 5
    for pivot in range(4, -1, -1):
        value = target[pivot]
        for right in range(pivot + 1, 5):
            value = value - matrix[pivot][right] * result[right]
        result[pivot] = value / matrix[pivot][pivot]
    return jnp.stack(result, 0)


def knot_rows(basis_rows, knot_first, squared):
    knots = knot_first.shape[0]
    positions = jnp.arange(KNOT, dtype=jnp.int32)[None, :]
    total = jnp.zeros((knots, KNOT), jnp.float32)
    for offset in range(4):
        value = basis_rows[:, offset]
        if squared:
            value = value * value
        total = total + jnp.where(
            positions == knot_first[:, None] + offset, value[:, None], jnp.float32(0.0)
        )
    return total


def on_device(
    residual,
    weight,
    source_part,
    attitude_part,
    calib_part,
    phase,
    obs_source,
    obs_owner,
    obs_slot,
    obs_knot,
    obs_calib,
    tile_count,
    time_list,
):
    count = residual.shape[0]
    devices = lax.axis_size(("src", "att"))
    tiles = tile_count.shape[1]
    index = jnp.arange(count, dtype=jnp.int32)
    live = (index % OBS_TILE).reshape(tiles, OBS_TILE) < tile_count.reshape(tiles, 1)
    weighted = jnp.where(live.reshape(count), weight, jnp.float32(0.0))
    onehot = (
        obs_source.reshape(tiles, OBS_TILE)[:, :, None]
        == jnp.arange(SRC_TILE, dtype=jnp.int32)[None, None, :]
    ).astype(jnp.float32)
    columns = []
    for left in range(5):
        for right in range(left, 5):
            columns.append(weighted * source_part[left] * source_part[right])
    for left in range(5):
        columns.append(weighted * source_part[left] * residual)
    stacked = jnp.stack(columns, 0).reshape(20, tiles, OBS_TILE)
    sums = jnp.einsum(
        "tos,cto->tsc", onehot, stacked, precision=HIGH, preferred_element_type=jnp.float32
    )
    source_update = solve_normals(sums.reshape(tiles * SRC_TILE, 20))
    per_obs = jnp.einsum(
        "tos,kts->kto",
        onehot,
        source_update.reshape(5, tiles, SRC_TILE),
        precision=HIGH,
        preferred_element_type=jnp.float32,
    )
    first = residual - jnp.sum(source_part * per_obs.reshape(5, count), axis=0)
    basis_rows = jnp.stack(spline_weights(phase), 1)
    attitude_rows = attitude_part.T
    listed_blocks = devices * LIST
    block_id = obs_owner * LIST + obs_slot
    rhs_terms = weighted[:, None] * attitude_rows * first[:, None]
    diag_terms = weighted[:, None] * attitude_rows * attitude_rows
    calib_terms_obs = jnp.stack(
        [weighted * calib_part * first, weighted * calib_part * calib_part], 1
    )
    step_rows = math.gcd(count, 2048)
    steps = count // step_rows
    block_ids = jnp.arange(listed_blocks, dtype=jnp.int32)[None, :]
    calib_ids = jnp.arange(NCAL, dtype=jnp.int32)[None, :]

    def accumulate(carry, inputs):
        partial_value, calib_sum = carry
        blocks, knot_first, basis_part, rhs_part, diag_part, calib_ids_part, calib_vals = inputs
        linear = knot_rows(basis_part, knot_first, False)
        squares = knot_rows(basis_part, knot_first, True)
        spread = jnp.concatenate(
            [
                linear[:, :, None] * rhs_part[:, None, :],
                squares[:, :, None] * diag_part[:, None, :],
            ],
            axis=2,
        )
        spread = spread.reshape(step_rows, KNOT * 8)
        selector = (blocks[:, None] == block_ids).astype(jnp.float32)
        partial_value = partial_value + jnp.einsum(
            "ib,im->bm", selector, spread, precision=HIGH, preferred_element_type=jnp.float32
        )
        calib_hot = (calib_ids_part[:, None] == calib_ids).astype(jnp.float32)
        calib_sum = calib_sum + jnp.einsum(
            "in,ic->cn", calib_hot, calib_vals, precision=HIGH, preferred_element_type=jnp.float32
        )
        return ((partial_value, calib_sum), None)

    inputs = (
        block_id.reshape(steps, step_rows),
        obs_knot.reshape(steps, step_rows),
        basis_rows.reshape(steps, step_rows, 4),
        rhs_terms.reshape(steps, step_rows, 4),
        diag_terms.reshape(steps, step_rows, 4),
        obs_calib.reshape(steps, step_rows),
        calib_terms_obs.reshape(steps, step_rows, 2),
    )
    start = (jnp.zeros((listed_blocks, KNOT * 8), jnp.float32), jnp.zeros((2, NCAL), jnp.float32))
    (partial_value, calib_terms), _ = lax.scan(accumulate, start, inputs)
    outgoing = partial_value.reshape(devices, LIST, KNOT * 8)
    arrived = lax.all_to_all(outgoing, ("src", "att"), split_axis=0, concat_axis=0, tiled=True)
    totals = lax.psum(calib_terms, ("src", "att"))
    calib_update = totals[0] / (totals[1] + 1.0)
    listed = time_list.reshape(devices * LIST)
    selector = (listed[None, :] == jnp.arange(KB_DEV, dtype=jnp.int32)[:, None]).astype(jnp.float32)
    owned = jnp.dot(
        selector,
        arrived.reshape(devices * LIST, KNOT * 8),
        precision=HIGH,
        preferred_element_type=jnp.float32,
    )
    owned = owned.reshape(KB_DEV, KNOT, 8)
    update = owned[:, :, 0:4] / (owned[:, :, 4:8] + 1.0)
    attitude_update = update.reshape(KB_DEV * KNOT, 4).T
    returning = jnp.dot(
        selector.T,
        update.reshape(KB_DEV, KNOT * 4),
        precision=HIGH,
        preferred_element_type=jnp.float32,
    )
    returning = returning.reshape(devices, LIST, KNOT * 4)
    segment = lax.all_to_all(returning, ("src", "att"), split_axis=0, concat_axis=0, tiled=True)
    segment_rows = segment.reshape(listed_blocks, KNOT * 4)

    def correct(carry, inputs):
        blocks, knot_first, basis_part, attitude_block, calib_ids_part, calib_coef, first_part = (
            inputs
        )
        selector_rows = (blocks[:, None] == block_ids).astype(jnp.float32)
        fetched = jnp.dot(
            selector_rows, segment_rows, precision=HIGH, preferred_element_type=jnp.float32
        )
        fetched = fetched.reshape(step_rows, KNOT, 4)
        projected = jnp.sum(fetched * attitude_block[:, None, :], axis=2)
        linear = knot_rows(basis_part, knot_first, False)
        attitude_term = jnp.sum(linear * projected, axis=1)
        calib_hot = (calib_ids_part[:, None] == calib_ids).astype(jnp.float32)
        calib_value = jnp.dot(
            calib_hot, calib_update, precision=HIGH, preferred_element_type=jnp.float32
        )
        return (carry, first_part - attitude_term - calib_coef * calib_value)

    inputs_back = (
        block_id.reshape(steps, step_rows),
        obs_knot.reshape(steps, step_rows),
        basis_rows.reshape(steps, step_rows, 4),
        attitude_rows.reshape(steps, step_rows, 4),
        obs_calib.reshape(steps, step_rows),
        calib_part.reshape(steps, step_rows),
        first.reshape(steps, step_rows),
    )
    _, residual_blocks = lax.scan(correct, jnp.float32(0.0), inputs_back)
    residual_out = residual_blocks.reshape(count)
    return (source_update, attitude_update, calib_update, residual_out)


def solution(mesh):
    placed = (
        P(("src", "att")),
        P(("src", "att")),
        P(None, ("src", "att")),
        P(None, ("src", "att")),
        P(("src", "att")),
        P(("src", "att")),
        P(("src", "att")),
        P(("src", "att")),
        P(("src", "att")),
        P(("src", "att")),
        P(("src", "att")),
        P(("src", "att"), None),
        P(None, ("src", "att"), None),
    )
    return jax.shard_map(
        on_device,
        mesh=mesh,
        in_specs=placed,
        out_specs=(P(None, ("src", "att")), P(None, ("src", "att")), P(), P(("src", "att"))),
        check_vma=False,
    )
```

profile of v0, /device:TPU:0, one launch (start us, length us, event | category | flops | bytes accessed | tf_op | source)
XLA Modules:
  0.0 256.5 jit_solution(3903458531358402341)
XLA Ops:
  1.4 1.9 fusion.111
  3.3 0.8 eq.285
  4.1 0.8 multiply_multiply_fusion.6
  4.9 0.8 multiply_multiply_fusion.8
  5.7 1.0 stack.117
  6.7 1.1 fusion.27
  9.9 0.7 fusion.26
  11.1 87.2 %while.25 = (s32[]{:T(128)}, f32[128,1024]{1,0:T(8,128)S(1)}, f32[2,2048]{1,0:T(2,128)S(1)}, s32[4,2048]{1,0:T(4,128)S(1)}, s32[4,2048]{1,0:T(4,128)S(1)}, /*ind...) while((s32[]{:T(128)}, f32[128,1024]{1,0:T(8,128)S(1)}, ...), condition=%wide.region_2.3_spmd.clone, body=%wide.region_1.2_spmd.clone.sunk | while | flops 3335804928 | bytes 22626460 | solution.py:159
  12.1 3.1 %broadcast_multiply_fusion.4 = f32[2048,128,4]{0,2,1:T(4,128)} fusion(f32[2048,4]{0,1:T(4,128)S(1)} %get-tuple-element.550, f32[2048,128]{0,1:T(8,128)S(1)} %get-tuple-element.563), kind=kLoop, calls=%fused_computation.35.clone.1 | loop fusion | flops 1048576 | bytes 5275648 | tf_op jit(solution)/shard_map/while/body/eval_jaxpr/mul | solution.py:134
  15.2 3.2 %broadcast_multiply_fusion.5 = f32[2048,128,4]{0,2,1:T(4,128)} fusion(f32[2048,4]{0,1:T(4,128)S(1)} %get-tuple-element.564, f32[2048,128]{0,1:T(8,128)S(1)} %get-tuple-element.565), kind=kLoop, calls=%fused_computation.36.clone.1 | loop fusion | flops 1048576 | bytes 5275648 | tf_op jit(solution)/shard_map/while/body/eval_jaxpr/mul | solution.py:133
  18.4 9.3 %fusion.136 = f32[128,1024]{1,0:T(8,128)S(1)} fusion(f32[2048,128,4]{0,2,1:T(4,128)} %broadcast_multiply_fusion.4, f32[2048,128,4]{0,2,1:T(4,128)} %broadcast_multiply_fusion.5, f32[128,1024]{1,0:T(8,128)S(1)} %get-tuple-element.580, s32[2048]{0:T(1024)S(1)} %bitcast.454, pred[]{:T(512)S(6)} %compare.4), kind=kOutput, calls=%fused_computation.37.clone.1 | convolution fusion | flops 3224109056 | bytes 9445377 | tf_op jit(solution)/shard_map/while/body/eval_jaxpr/ib,im->bm/dot_general | solution.py:140
  27.7 5.4 %fusion.137 = f32[2,2048]{1,0:T(2,128)S(1)} fusion(s32[2048]{0:T(1024)S(1)} %bitcast.470, f32[2,2048]{1,0:T(2,128)S(1)} %get-tuple-element.581, f32[4,2048,2]{1,2,0:T(2,128)S(1)} %get-tuple-element.599, s32[]{:T(128)S(6)} %copy.66, pred[]{:T(512)S(6)} %compare.4), kind=kOutput, calls=%fused_computation.34.clone.1 | convolution fusion | flops 104865792 | bytes 57349 | tf_op jit(solution)/shard_map/while/body/eval_jaxpr/in,ic->cn/dot_general | solution.py:144
  33.8 3.1 %broadcast_multiply_fusion.4 = f32[2048,128,4]{0,2,1:T(4,128)} fusion(f32[2048,4]{0,1:T(4,128)S(1)} %get-tuple-element.550, f32[2048,128]{0,1:T(8,128)S(1)} %get-tuple-element.563), kind=kLoop, calls=%fused_computation.35.clone.1 | loop fusion | flops 1048576 | bytes 5275648 | tf_op jit(solution)/shard_map/while/body/eval_jaxpr/mul | solution.py:134
  36.9 3.2 %broadcast_multiply_fusion.5 = f32[2048,128,4]{0,2,1:T(4,128)} fusion(f32[2048,4]{0,1:T(4,128)S(1)} %get-tuple-element.564, f32[2048,128]{0,1:T(8,128)S(1)} %get-tuple-element.565), kind=kLoop, calls=%fused_computation.36.clone.1 | loop fusion | flops 1048576 | bytes 5275648 | tf_op jit(solution)/shard_map/while/body/eval_jaxpr/mul | solution.py:133
  40.1 9.3 %fusion.136 = f32[128,1024]{1,0:T(8,128)S(1)} fusion(f32[2048,128,4]{0,2,1:T(4,128)} %broadcast_multiply_fusion.4, f32[2048,128,4]{0,2,1:T(4,128)} %broadcast_multiply_fusion.5, f32[128,1024]{1,0:T(8,128)S(1)} %get-tuple-element.580, s32[2048]{0:T(1024)S(1)} %bitcast.454, pred[]{:T(512)S(6)} %compare.4), kind=kOutput, calls=%fused_computation.37.clone.1 | convolution fusion | flops 3224109056 | bytes 9445377 | tf_op jit(solution)/shard_map/while/body/eval_jaxpr/ib,im->bm/dot_general | solution.py:140
  49.4 5.4 %fusion.137 = f32[2,2048]{1,0:T(2,128)S(1)} fusion(s32[2048]{0:T(1024)S(1)} %bitcast.470, f32[2,2048]{1,0:T(2,128)S(1)} %get-tuple-element.581, f32[4,2048,2]{1,2,0:T(2,128)S(1)} %get-tuple-element.599, s32[]{:T(128)S(6)} %copy.66, pred[]{:T(512)S(6)} %compare.4), kind=kOutput, calls=%fused_computation.34.clone.1 | convolution fusion | flops 104865792 | bytes 57349 | tf_op jit(solution)/shard_map/while/body/eval_jaxpr/in,ic->cn/dot_general | solution.py:144
  55.5 3.1 %broadcast_multiply_fusion.4 = f32[2048,128,4]{0,2,1:T(4,128)} fusion(f32[2048,4]{0,1:T(4,128)S(1)} %get-tuple-element.550, f32[2048,128]{0,1:T(8,128)S(1)} %get-tuple-element.563), kind=kLoop, calls=%fused_computation.35.clone.1 | loop fusion | flops 1048576 | bytes 5275648 | tf_op jit(solution)/shard_map/while/body/eval_jaxpr/mul | solution.py:134
  58.6 3.2 %broadcast_multiply_fusion.5 = f32[2048,128,4]{0,2,1:T(4,128)} fusion(f32[2048,4]{0,1:T(4,128)S(1)} %get-tuple-element.564, f32[2048,128]{0,1:T(8,128)S(1)} %get-tuple-element.565), kind=kLoop, calls=%fused_computation.36.clone.1 | loop fusion | flops 1048576 | bytes 5275648 | tf_op jit(solution)/shard_map/while/body/eval_jaxpr/mul | solution.py:133
  61.8 9.3 %fusion.136 = f32[128,1024]{1,0:T(8,128)S(1)} fusion(f32[2048,128,4]{0,2,1:T(4,128)} %broadcast_multiply_fusion.4, f32[2048,128,4]{0,2,1:T(4,128)} %broadcast_multiply_fusion.5, f32[128,1024]{1,0:T(8,128)S(1)} %get-tuple-element.580, s32[2048]{0:T(1024)S(1)} %bitcast.454, pred[]{:T(512)S(6)} %compare.4), kind=kOutput, calls=%fused_computation.37.clone.1 | convolution fusion | flops 3224109056 | bytes 9445377 | tf_op jit(solution)/shard_map/while/body/eval_jaxpr/ib,im->bm/dot_general | solution.py:140
  71.1 5.4 %fusion.137 = f32[2,2048]{1,0:T(2,128)S(1)} fusion(s32[2048]{0:T(1024)S(1)} %bitcast.470, f32[2,2048]{1,0:T(2,128)S(1)} %get-tuple-element.581, f32[4,2048,2]{1,2,0:T(2,128)S(1)} %get-tuple-element.599, s32[]{:T(128)S(6)} %copy.66, pred[]{:T(512)S(6)} %compare.4), kind=kOutput, calls=%fused_computation.34.clone.1 | convolution fusion | flops 104865792 | bytes 57349 | tf_op jit(solution)/shard_map/while/body/eval_jaxpr/in,ic->cn/dot_general | solution.py:144
  77.2 3.1 %broadcast_multiply_fusion.4 = f32[2048,128,4]{0,2,1:T(4,128)} fusion(f32[2048,4]{0,1:T(4,128)S(1)} %get-tuple-element.550, f32[2048,128]{0,1:T(8,128)S(1)} %get-tuple-element.563), kind=kLoop, calls=%fused_computation.35.clone.1 | loop fusion | flops 1048576 | bytes 5275648 | tf_op jit(solution)/shard_map/while/body/eval_jaxpr/mul | solution.py:134
  80.4 3.2 %broadcast_multiply_fusion.5 = f32[2048,128,4]{0,2,1:T(4,128)} fusion(f32[2048,4]{0,1:T(4,128)S(1)} %get-tuple-element.564, f32[2048,128]{0,1:T(8,128)S(1)} %get-tuple-element.565), kind=kLoop, calls=%fused_computation.36.clone.1 | loop fusion | flops 1048576 | bytes 5275648 | tf_op jit(solution)/shard_map/while/body/eval_jaxpr/mul | solution.py:133
  83.5 9.3 %fusion.136 = f32[128,1024]{1,0:T(8,128)S(1)} fusion(f32[2048,128,4]{0,2,1:T(4,128)} %broadcast_multiply_fusion.4, f32[2048,128,4]{0,2,1:T(4,128)} %broadcast_multiply_fusion.5, f32[128,1024]{1,0:T(8,128)S(1)} %get-tuple-element.580, s32[2048]{0:T(1024)S(1)} %bitcast.454, pred[]{:T(512)S(6)} %compare.4), kind=kOutput, calls=%fused_computation.37.clone.1 | convolution fusion | flops 3224109056 | bytes 9445377 | tf_op jit(solution)/shard_map/while/body/eval_jaxpr/ib,im->bm/dot_general | solution.py:140
  92.8 5.4 %fusion.137 = f32[2,2048]{1,0:T(2,128)S(1)} fusion(s32[2048]{0:T(1024)S(1)} %bitcast.470, f32[2,2048]{1,0:T(2,128)S(1)} %get-tuple-element.581, f32[4,2048,2]{1,2,0:T(2,128)S(1)} %get-tuple-element.599, s32[]{:T(128)S(6)} %copy.66, pred[]{:T(512)S(6)} %compare.4), kind=kOutput, calls=%fused_computation.34.clone.1 | convolution fusion | flops 104865792 | bytes 57349 | tf_op jit(solution)/shard_map/while/body/eval_jaxpr/in,ic->cn/dot_general | solution.py:144
  98.3 0.9 reshape.3148
  99.3 7.3 %all-to-all-start = ((f32[32,4,1024]{2,1,0:T(4,128)}), f32[32,4,1024]{2,1,0:T(4,128)S(1)}, u32[]{:S(2)}, u32[]{:S(2)}) async-start(f32[32,4,1024]{2,1,0:T(4,128)} %reshape.3148), calls=%async_computation | async-start | bytes 1048576 | tf_op jit(solution)/shard_map/all_to_all | solution.py:161
  106.9 0.6 stack.118
  107.6 40.8 %psum.7 = f32[2,2048]{1,0:T(2,128)S(1)} all-reduce(f32[2,2048]{1,0:T(2,128)S(1)} %get-tuple-element.135), channel_id=1, replica_groups=mesh['src'=8,'att'=4] {'src','att'}, use_global_device_ids=true, to_apply=%region_3.4 | all-reduce | flops 4096 | bytes 32768 | tf_op jit(solution)/shard_map/psum | solution.py:162
  149.7 0.9 copy.46
  150.5 4.4 %all-to-all-start.1 = ((f32[32,4,512]{2,1,0:T(4,128)}), f32[32,4,512]{2,1,0:T(4,128)S(1)}, u32[]{:S(2)}, u32[]{:S(2)}) async-start(f32[32,4,512]{2,1,0:T(4,128)} %copy.46), calls=%async_computation.1 | async-start | bytes 524288 | tf_op jit(solution)/shard_map/all_to_all | solution.py:182
  155.6 9.9 %all-to-all-done.1 = f32[32,4,512]{2,1,0:T(4,128)S(1)} async-done(((f32[32,4,512]{2,1,0:T(4,128)}), f32[32,4,512]{2,1,0:T(4,128)S(1)}, u32[]{:S(2)}, u32[]{:S(2)}) %all-to-all-start.1) | async-done | bytes 262176 | tf_op jit(solution)/shard_map/all_to_all | solution.py:182
  165.7 90.2 %while.24 = (s32[]{:T(128)}, f32[4,2048]{1,0:T(4,128)S(1)}, f32[4,2048]{1,0:T(4,128)S(1)}, s32[4,2048]{1,0:T(4,128)S(1)}, f32[4,2048,4]{1,2,0:T(4,128)S(1)}, /*i...) while((s32[]{:T(128)}, f32[4,2048]{1,0:T(4,128)S(1)}, ...), condition=%wide.region_7.8_spmd.clone, body=%wide.region_4.7_spmd.clone.sunk | while | flops 1670653952 | bytes 19644568 | solution.py:212
  165.7 7.5 %fusion.130 = f32[1,2048]{1,0:T(1,128)S(1)} fusion(f32[2048,1]{0,1:T(1,128)S(1)} %bitcast.504, s32[2048]{0:T(1024)S(1)} %bitcast.471), kind=kOutput, calls=%fused_computation.5.clone.1 | convolution fusion | flops 54525952 | bytes 24576 | tf_op jit(solution)/shard_map/while/body/eval_jaxpr/dot_general | solution.py:198
  173.3 3.7 %fusion.131 = f32[2048,512]{0,1:T(8,128)} fusion(f32[128,512]{1,0:T(8,128)S(1)} %get-tuple-element.635, s32[2048]{0:T(1024)S(1)} %bitcast.446), kind=kOutput, calls=%fused_computation.14.clone.1 | convolution fusion | flops 1610874880 | bytes 4464640 | tf_op jit(solution)/shard_map/while/body/eval_jaxpr/dot_general | solution.py:190
  177.0 5.2 %reshape.3266 = f32[2048,128,4]{0,2,1:T(4,128)} reshape(f32[2048,512]{0,1:T(8,128)} %fusion.131) | data formatting | bytes 8388608 | tf_op jit(solution)/shard_map/while/body/eval_jaxpr/reshape | solution.py:193
  182.2 5.3 %multiply_reduce_fusion.5 = f32[2048,128]{0,1:T(8,128)S(1)} fusion(f32[2048,128,4]{0,2,1:T(4,128)} %reshape.3266, f32[2048,4]{0,1:T(4,128)S(1)} %get-tuple-element.531), kind=kLoop, calls=%fused_computation.7.clone.1 | loop fusion | flops 1835008 | bytes 5275648 | tf_op jit(solution)/shard_map/while/body/eval_jaxpr/reduce_sum | solution.py:194
  188.3 7.5 %fusion.130 = f32[1,2048]{1,0:T(1,128)S(1)} fusion(f32[2048,1]{0,1:T(1,128)S(1)} %bitcast.504, s32[2048]{0:T(1024)S(1)} %bitcast.471), kind=kOutput, calls=%fused_computation.5.clone.1 | convolution fusion | flops 54525952 | bytes 24576 | tf_op jit(solution)/shard_map/while/body/eval_jaxpr/dot_general | solution.py:198
  195.8 3.7 %fusion.131 = f32[2048,512]{0,1:T(8,128)} fusion(f32[128,512]{1,0:T(8,128)S(1)} %get-tuple-element.635, s32[2048]{0:T(1024)S(1)} %bitcast.446), kind=kOutput, calls=%fused_computation.14.clone.1 | convolution fusion | flops 1610874880 | bytes 4464640 | tf_op jit(solution)/shard_map/while/body/eval_jaxpr/dot_general | solution.py:190
  199.6 5.2 %reshape.3266 = f32[2048,128,4]{0,2,1:T(4,128)} reshape(f32[2048,512]{0,1:T(8,128)} %fusion.131) | data formatting | bytes 8388608 | tf_op jit(solution)/shard_map/while/body/eval_jaxpr/reshape | solution.py:193
  204.7 5.3 %multiply_reduce_fusion.5 = f32[2048,128]{0,1:T(8,128)S(1)} fusion(f32[2048,128,4]{0,2,1:T(4,128)} %reshape.3266, f32[2048,4]{0,1:T(4,128)S(1)} %get-tuple-element.531), kind=kLoop, calls=%fused_computation.7.clone.1 | loop fusion | flops 1835008 | bytes 5275648 | tf_op jit(solution)/shard_map/while/body/eval_jaxpr/reduce_sum | solution.py:194
  210.8 7.5 %fusion.130 = f32[1,2048]{1,0:T(1,128)S(1)} fusion(f32[2048,1]{0,1:T(1,128)S(1)} %bitcast.504, s32[2048]{0:T(1024)S(1)} %bitcast.471), kind=kOutput, calls=%fused_computation.5.clone.1 | convolution fusion | flops 54525952 | bytes 24576 | tf_op jit(solution)/shard_map/while/body/eval_jaxpr/dot_general | solution.py:198
  218.3 3.7 %fusion.131 = f32[2048,512]{0,1:T(8,128)} fusion(f32[128,512]{1,0:T(8,128)S(1)} %get-tuple-element.635, s32[2048]{0:T(1024)S(1)} %bitcast.446), kind=kOutput, calls=%fused_computation.14.clone.1 | convolution fusion | flops 1610874880 | bytes 4464640 | tf_op jit(solution)/shard_map/while/body/eval_jaxpr/dot_general | solution.py:190
  222.1 5.2 %reshape.3266 = f32[2048,128,4]{0,2,1:T(4,128)} reshape(f32[2048,512]{0,1:T(8,128)} %fusion.131) | data formatting | bytes 8388608 | tf_op jit(solution)/shard_map/while/body/eval_jaxpr/reshape | solution.py:193
  227.3 5.3 %multiply_reduce_fusion.5 = f32[2048,128]{0,1:T(8,128)S(1)} fusion(f32[2048,128,4]{0,2,1:T(4,128)} %reshape.3266, f32[2048,4]{0,1:T(4,128)S(1)} %get-tuple-element.531), kind=kLoop, calls=%fused_computation.7.clone.1 | loop fusion | flops 1835008 | bytes 5275648 | tf_op jit(solution)/shard_map/while/body/eval_jaxpr/reduce_sum | solution.py:194
  233.4 7.5 %fusion.130 = f32[1,2048]{1,0:T(1,128)S(1)} fusion(f32[2048,1]{0,1:T(1,128)S(1)} %bitcast.504, s32[2048]{0:T(1024)S(1)} %bitcast.471), kind=kOutput, calls=%fused_computation.5.clone.1 | convolution fusion | flops 54525952 | bytes 24576 | tf_op jit(solution)/shard_map/while/body/eval_jaxpr/dot_general | solution.py:198
  240.9 3.7 %fusion.131 = f32[2048,512]{0,1:T(8,128)} fusion(f32[128,512]{1,0:T(8,128)S(1)} %get-tuple-element.635, s32[2048]{0:T(1024)S(1)} %bitcast.446), kind=kOutput, calls=%fused_computation.14.clone.1 | convolution fusion | flops 1610874880 | bytes 4464640 | tf_op jit(solution)/shard_map/while/body/eval_jaxpr/dot_general | solution.py:190
  244.6 5.2 %reshape.3266 = f32[2048,128,4]{0,2,1:T(4,128)} reshape(f32[2048,512]{0,1:T(8,128)} %fusion.131) | data formatting | bytes 8388608 | tf_op jit(solution)/shard_map/while/body/eval_jaxpr/reshape | solution.py:193
  249.8 5.3 %multiply_reduce_fusion.5 = f32[2048,128]{0,1:T(8,128)S(1)} fusion(f32[2048,128,4]{0,2,1:T(4,128)} %reshape.3266, f32[2048,4]{0,1:T(4,128)S(1)} %get-tuple-element.531), kind=kLoop, calls=%fused_computation.7.clone.1 | loop fusion | flops 1835008 | bytes 5275648 | tf_op jit(solution)/shard_map/while/body/eval_jaxpr/reduce_sum | solution.py:194
  (154 shorter events, 11.6 us)
Async XLA Ops:
  0.6 0.7 copy-start
  0.6 10.0 %copy-start.1 = (f32[5,8192]{1,0:T(8,128)S(1)}, f32[5,8192]{1,0:T(8,128)}, u32[]{:S(2)}) copy-start(f32[5,8192]{1,0:T(8,128)} %param.19) | copy-start | bytes 491524
  0.7 10.1 %copy-start.3 = (f32[8192]{0:T(1024)S(1)}, f32[8192]{0:T(1024)}, u32[]{:S(2)}) copy-start(f32[8192]{0:T(1024)} %param.21) | copy-start | bytes 98308
  0.7 10.1 %copy-start.4 = (f32[8192]{0:T(1024)S(1)}, f32[8192]{0:T(1024)}, u32[]{:S(2)}) copy-start(f32[8192]{0:T(1024)} %param.17) | copy-start | bytes 98308
  0.7 7.3 %copy-start.5 = (s32[8192]{0:T(1024)S(1)}, s32[8192]{0:T(1024)}, u32[]{:S(2)}) copy-start(s32[8192]{0:T(1024)} %param.25) | copy-start | bytes 98308
  0.7 7.3 %copy-start.6 = (s32[8192]{0:T(1024)S(1)}, s32[8192]{0:T(1024)}, u32[]{:S(2)}) copy-start(s32[8192]{0:T(1024)} %param.24) | copy-start | bytes 98308
  0.7 7.4 %copy-start.8 = (s32[8192]{0:T(1024)S(1)}, s32[8192]{0:T(1024)}, u32[]{:S(2)}) copy-start(s32[8192]{0:T(1024)} %param.26) | copy-start | bytes 98308
  0.7 7.4 %copy-start.7 = (f32[8192]{0:T(1024)S(1)}, f32[8192]{0:T(1024)}, u32[]{:S(2)}) copy-start(f32[8192]{0:T(1024)} %param.22) | copy-start | bytes 98308
  0.7 10.1 %copy-start.9 = (s32[8192]{0:T(1024)S(1)}, s32[8192]{0:T(1024)}, u32[]{:S(2)}) copy-start(s32[8192]{0:T(1024)} %param.27) | copy-start | bytes 98308
  0.7 10.1 %copy-start.2 = (f32[4,8192]{1,0:T(4,128)S(1)}, f32[4,8192]{1,0:T(4,128)}, u32[]{:S(2)}) copy-start(f32[4,8192]{1,0:T(4,128)} %param.20) | copy-start | bytes 393220
  11.1 95.5 %copy-start.10 = (s32[32,1,4]{0,2,1:T(4,128)S(1)}, s32[32,1,4]{0,2,1:T(4,128)}, u32[]{:S(2)}) copy-start(s32[32,1,4]{0,2,1:T(4,128)} %param.29) | copy-start | bytes 1540
  99.3 49.1 %all-to-all-start = ((f32[32,4,1024]{2,1,0:T(4,128)}), f32[32,4,1024]{2,1,0:T(4,128)S(1)}, u32[]{:S(2)}, u32[]{:S(2)}) async-start(f32[32,4,1024]{2,1,0:T(4,128)} %reshape.3148), calls=%async_computation | async-start | bytes 1048576 | tf_op jit(solution)/shard_map/all_to_all | solution.py:161
  150.5 15.0 %all-to-all-start.1 = ((f32[32,4,512]{2,1,0:T(4,128)}), f32[32,4,512]{2,1,0:T(4,128)S(1)}, u32[]{:S(2)}, u32[]{:S(2)}) async-start(f32[32,4,512]{2,1,0:T(4,128)} %copy.46), calls=%async_computation.1 | async-start | bytes 524288 | tf_op jit(solution)/shard_map/all_to_all | solution.py:182
  255.9 0.6 copy-start.11
where the time goes:
time: 258 us; the launch traced here: 256 us
  matrix products  106 us (41%)
  other arithmetic  53.4 us (21%)
  blocking collectives  40.8 us (16%)
  local copies, waits for them, and re-layouts  32.3 us (13%)
  starting transfers between devices  11.7 us (5%)
  waiting for transfers between devices  9.94 us (4%)
    psum x1, blocking collectives, on_device(): totals = lax.psum(calib_terms, ('src', 'att'))  40.8 us
    dot_general x4, matrix products, accumulate(): jnp.einsum('ib,im->bm', selector, spread, precision=HIGH, preferred_eleme...  37.2 us
    dot_general x4, matrix products, correct(): jnp.dot(calib_hot, calib_update, precision=HIGH, preferred_element_type=j...  30.1 us
    dot_general x4, matrix products, accumulate(): jnp.einsum('in,ic->cn', calib_hot, calib_vals, precision=HIGH, preferred_...  21.4 us
    reduce_sum x4, other arithmetic, correct(): projected = jnp.sum(fetched * attitude_block[:, None, :], axis=2)  21.3 us
    reshape x4, local copies, waits for them, and re-layouts, correct(): fetched = fetched.reshape(step_rows, KNOT, 4)  20.7 us
    dot_general x4, matrix products, correct(): jnp.dot(selector_rows, segment_rows, precision=HIGH, preferred_element_ty...  15 us
    mul x4, other arithmetic, accumulate(): linear[:, :, None] * rhs_part[:, None, :]  12.7 us
  transfers between devices with their start and end apart: 2, of which 1 were waited for; matrix products, arithmetic and copies ran while one was open for 1% of the time, Pallas kernels for 0%

commit v1 on v0

--- a/solution.py
+++ b/solution.py
@@ -159,7 +159,7 @@
     (partial_value, calib_terms), _ = lax.scan(accumulate, start, inputs)
     outgoing = partial_value.reshape(devices, LIST, KNOT * 8)
     arrived = lax.all_to_all(outgoing, ("src", "att"), split_axis=0, concat_axis=0, tiled=True)
-    totals = lax.psum(calib_terms, ("src", "att"))
+    totals = jnp.sum(lax.all_gather(calib_terms, ("src", "att")), axis=0)
     calib_update = totals[0] / (totals[1] + 1.0)
     listed = time_list.reshape(devices * LIST)
     selector = (listed[None, :] == jnp.arange(KB_DEV, dtype=jnp.int32)[:, None]).astype(jnp.float32)

time: 258 us -> 260 us (level)
  blocking collectives: 40.8 us -> 45.2 us
    all_gather x0 -> x1, blocking collectives: none -> 45.2 us  [on_device(): totals = jnp.sum(lax.all_gather(calib_terms, ('src', 'att')), axis=0)]
    psum x1 -> x0, blocking collectives: 40.8 us -> none  [on_device(): totals = lax.psum(calib_terms, ('src', 'att'))]
where the time goes in v1:
time: 260 us; the launch traced here: 259 us
  matrix products  106 us (41%)
  other arithmetic  53.6 us (21%)
  blocking collectives  45.2 us (17%)
  local copies, waits for them, and re-layouts  32.3 us (12%)
  waiting for transfers between devices  9.94 us (4%)
  starting transfers between devices  9.88 us (4%)
    all_gather x1, blocking collectives, on_device(): totals = jnp.sum(lax.all_gather(calib_terms, ('src', 'att')), axis=0)  45.2 us
    dot_general x4, matrix products, accumulate(): jnp.einsum('ib,im->bm', selector, spread, precision=HIGH, preferred_eleme...  37.2 us
    dot_general x4, matrix products, correct(): jnp.dot(calib_hot, calib_update, precision=HIGH, preferred_element_type=j...  30.1 us
    dot_general x4, matrix products, accumulate(): jnp.einsum('in,ic->cn', calib_hot, calib_vals, precision=HIGH, preferred_...  21.4 us
    reduce_sum x4, other arithmetic, correct(): projected = jnp.sum(fetched * attitude_block[:, None, :], axis=2)  21.3 us
    reshape x4, local copies, waits for them, and re-layouts, correct(): fetched = fetched.reshape(step_rows, KNOT, 4)  20.7 us
    dot_general x4, matrix products, correct(): jnp.dot(selector_rows, segment_rows, precision=HIGH, preferred_element_ty...  15 us
    mul x4, other arithmetic, accumulate(): linear[:, :, None] * rhs_part[:, None, :]  12.7 us
  transfers between devices with their start and end apart: 2, of which 1 were waited for; matrix products, arithmetic and copies ran while one was open for 1% of the time, Pallas kernels for 0%

profile of v1, /device:TPU:0, one launch (start us, length us, event | category | flops | bytes accessed | tf_op | source)
XLA Modules:
  0.0 259.1 jit_solution(3131968893809487225)
XLA Ops:
  1.4 1.9 fusion.111
  3.3 0.8 eq.285
  4.1 0.8 multiply_multiply_fusion.6
  4.9 0.8 multiply_multiply_fusion.8
  5.7 1.0 stack.117
  6.7 1.1 fusion.27
  9.9 0.7 fusion.26
  11.1 87.2 %while.25 = (s32[]{:T(128)}, f32[128,1024]{1,0:T(8,128)S(1)}, f32[2,2048]{1,0:T(2,128)S(1)}, s32[4,2048]{1,0:T(4,128)S(1)}, s32[4,2048]{1,0:T(4,128)S(1)}, /*ind...) while((s32[]{:T(128)}, f32[128,1024]{1,0:T(8,128)S(1)}, ...), condition=%wide.region_2.3_spmd.clone, body=%wide.region_1.2_spmd.clone.sunk | while | flops 3335804928 | bytes 22626460 | solution.py:159
  12.1 3.1 %broadcast_multiply_fusion.4 = f32[2048,128,4]{0,2,1:T(4,128)} fusion(f32[2048,4]{0,1:T(4,128)S(1)} %get-tuple-element.550, f32[2048,128]{0,1:T(8,128)S(1)} %get-tuple-element.563), kind=kLoop, calls=%fused_computation.35.clone.1 | loop fusion | flops 1048576 | bytes 5275648 | tf_op jit(solution)/shard_map/while/body/eval_jaxpr/mul | solution.py:134
  15.2 3.2 %broadcast_multiply_fusion.5 = f32[2048,128,4]{0,2,1:T(4,128)} fusion(f32[2048,4]{0,1:T(4,128)S(1)} %get-tuple-element.564, f32[2048,128]{0,1:T(8,128)S(1)} %get-tuple-element.565), kind=kLoop, calls=%fused_computation.36.clone.1 | loop fusion | flops 1048576 | bytes 5275648 | tf_op jit(solution)/shard_map/while/body/eval_jaxpr/mul | solution.py:133
  18.4 9.3 %fusion.136 = f32[128,1024]{1,0:T(8,128)S(1)} fusion(f32[2048,128,4]{0,2,1:T(4,128)} %broadcast_multiply_fusion.4, f32[2048,128,4]{0,2,1:T(4,128)} %broadcast_multiply_fusion.5, f32[128,1024]{1,0:T(8,128)S(1)} %get-tuple-element.580, s32[2048]{0:T(1024)S(1)} %bitcast.455, pred[]{:T(512)S(6)} %compare.4), kind=kOutput, calls=%fused_computation.37.clone.1 | convolution fusion | flops 3224109056 | bytes 9445377 | tf_op jit(solution)/shard_map/while/body/eval_jaxpr/ib,im->bm/dot_general | solution.py:140
  27.7 5.4 %fusion.137 = f32[2,2048]{1,0:T(2,128)S(1)} fusion(s32[2048]{0:T(1024)S(1)} %bitcast.471, f32[2,2048]{1,0:T(2,128)S(1)} %get-tuple-element.581, f32[4,2048,2]{1,2,0:T(2,128)S(1)} %get-tuple-element.599, s32[]{:T(128)S(6)} %copy.66, pred[]{:T(512)S(6)} %compare.4), kind=kOutput, calls=%fused_computation.34.clone.1 | convolution fusion | flops 104865792 | bytes 57349 | tf_op jit(solution)/shard_map/while/body/eval_jaxpr/in,ic->cn/dot_general | solution.py:144
  33.8 3.1 %broadcast_multiply_fusion.4 = f32[2048,128,4]{0,2,1:T(4,128)} fusion(f32[2048,4]{0,1:T(4,128)S(1)} %get-tuple-element.550, f32[2048,128]{0,1:T(8,128)S(1)} %get-tuple-element.563), kind=kLoop, calls=%fused_computation.35.clone.1 | loop fusion | flops 1048576 | bytes 5275648 | tf_op jit(solution)/shard_map/while/body/eval_jaxpr/mul | solution.py:134
  36.9 3.2 %broadcast_multiply_fusion.5 = f32[2048,128,4]{0,2,1:T(4,128)} fusion(f32[2048,4]{0,1:T(4,128)S(1)} %get-tuple-element.564, f32[2048,128]{0,1:T(8,128)S(1)} %get-tuple-element.565), kind=kLoop, calls=%fused_computation.36.clone.1 | loop fusion | flops 1048576 | bytes 5275648 | tf_op jit(solution)/shard_map/while/body/eval_jaxpr/mul | solution.py:133
  40.1 9.3 %fusion.136 = f32[128,1024]{1,0:T(8,128)S(1)} fusion(f32[2048,128,4]{0,2,1:T(4,128)} %broadcast_multiply_fusion.4, f32[2048,128,4]{0,2,1:T(4,128)} %broadcast_multiply_fusion.5, f32[128,1024]{1,0:T(8,128)S(1)} %get-tuple-element.580, s32[2048]{0:T(1024)S(1)} %bitcast.455, pred[]{:T(512)S(6)} %compare.4), kind=kOutput, calls=%fused_computation.37.clone.1 | convolution fusion | flops 3224109056 | bytes 9445377 | tf_op jit(solution)/shard_map/while/body/eval_jaxpr/ib,im->bm/dot_general | solution.py:140
  49.4 5.4 %fusion.137 = f32[2,2048]{1,0:T(2,128)S(1)} fusion(s32[2048]{0:T(1024)S(1)} %bitcast.471, f32[2,2048]{1,0:T(2,128)S(1)} %get-tuple-element.581, f32[4,2048,2]{1,2,0:T(2,128)S(1)} %get-tuple-element.599, s32[]{:T(128)S(6)} %copy.66, pred[]{:T(512)S(6)} %compare.4), kind=kOutput, calls=%fused_computation.34.clone.1 | convolution fusion | flops 104865792 | bytes 57349 | tf_op jit(solution)/shard_map/while/body/eval_jaxpr/in,ic->cn/dot_general | solution.py:144
  55.5 3.1 %broadcast_multiply_fusion.4 = f32[2048,128,4]{0,2,1:T(4,128)} fusion(f32[2048,4]{0,1:T(4,128)S(1)} %get-tuple-element.550, f32[2048,128]{0,1:T(8,128)S(1)} %get-tuple-element.563), kind=kLoop, calls=%fused_computation.35.clone.1 | loop fusion | flops 1048576 | bytes 5275648 | tf_op jit(solution)/shard_map/while/body/eval_jaxpr/mul | solution.py:134
  58.6 3.2 %broadcast_multiply_fusion.5 = f32[2048,128,4]{0,2,1:T(4,128)} fusion(f32[2048,4]{0,1:T(4,128)S(1)} %get-tuple-element.564, f32[2048,128]{0,1:T(8,128)S(1)} %get-tuple-element.565), kind=kLoop, calls=%fused_computation.36.clone.1 | loop fusion | flops 1048576 | bytes 5275648 | tf_op jit(solution)/shard_map/while/body/eval_jaxpr/mul | solution.py:133
  61.8 9.3 %fusion.136 = f32[128,1024]{1,0:T(8,128)S(1)} fusion(f32[2048,128,4]{0,2,1:T(4,128)} %broadcast_multiply_fusion.4, f32[2048,128,4]{0,2,1:T(4,128)} %broadcast_multiply_fusion.5, f32[128,1024]{1,0:T(8,128)S(1)} %get-tuple-element.580, s32[2048]{0:T(1024)S(1)} %bitcast.455, pred[]{:T(512)S(6)} %compare.4), kind=kOutput, calls=%fused_computation.37.clone.1 | convolution fusion | flops 3224109056 | bytes 9445377 | tf_op jit(solution)/shard_map/while/body/eval_jaxpr/ib,im->bm/dot_general | solution.py:140
  71.1 5.4 %fusion.137 = f32[2,2048]{1,0:T(2,128)S(1)} fusion(s32[2048]{0:T(1024)S(1)} %bitcast.471, f32[2,2048]{1,0:T(2,128)S(1)} %get-tuple-element.581, f32[4,2048,2]{1,2,0:T(2,128)S(1)} %get-tuple-element.599, s32[]{:T(128)S(6)} %copy.66, pred[]{:T(512)S(6)} %compare.4), kind=kOutput, calls=%fused_computation.34.clone.1 | convolution fusion | flops 104865792 | bytes 57349 | tf_op jit(solution)/shard_map/while/body/eval_jaxpr/in,ic->cn/dot_general | solution.py:144
  77.2 3.1 %broadcast_multiply_fusion.4 = f32[2048,128,4]{0,2,1:T(4,128)} fusion(f32[2048,4]{0,1:T(4,128)S(1)} %get-tuple-element.550, f32[2048,128]{0,1:T(8,128)S(1)} %get-tuple-element.563), kind=kLoop, calls=%fused_computation.35.clone.1 | loop fusion | flops 1048576 | bytes 5275648 | tf_op jit(solution)/shard_map/while/body/eval_jaxpr/mul | solution.py:134
  80.4 3.2 %broadcast_multiply_fusion.5 = f32[2048,128,4]{0,2,1:T(4,128)} fusion(f32[2048,4]{0,1:T(4,128)S(1)} %get-tuple-element.564, f32[2048,128]{0,1:T(8,128)S(1)} %get-tuple-element.565), kind=kLoop, calls=%fused_computation.36.clone.1 | loop fusion | flops 1048576 | bytes 5275648 | tf_op jit(solution)/shard_map/while/body/eval_jaxpr/mul | solution.py:133
  83.5 9.3 %fusion.136 = f32[128,1024]{1,0:T(8,128)S(1)} fusion(f32[2048,128,4]{0,2,1:T(4,128)} %broadcast_multiply_fusion.4, f32[2048,128,4]{0,2,1:T(4,128)} %broadcast_multiply_fusion.5, f32[128,1024]{1,0:T(8,128)S(1)} %get-tuple-element.580, s32[2048]{0:T(1024)S(1)} %bitcast.455, pred[]{:T(512)S(6)} %compare.4), kind=kOutput, calls=%fused_computation.37.clone.1 | convolution fusion | flops 3224109056 | bytes 9445377 | tf_op jit(solution)/shard_map/while/body/eval_jaxpr/ib,im->bm/dot_general | solution.py:140
  92.8 5.4 %fusion.137 = f32[2,2048]{1,0:T(2,128)S(1)} fusion(s32[2048]{0:T(1024)S(1)} %bitcast.471, f32[2,2048]{1,0:T(2,128)S(1)} %get-tuple-element.581, f32[4,2048,2]{1,2,0:T(2,128)S(1)} %get-tuple-element.599, s32[]{:T(128)S(6)} %copy.66, pred[]{:T(512)S(6)} %compare.4), kind=kOutput, calls=%fused_computation.34.clone.1 | convolution fusion | flops 104865792 | bytes 57349 | tf_op jit(solution)/shard_map/while/body/eval_jaxpr/in,ic->cn/dot_general | solution.py:144
  98.3 0.9 reshape.3148
  99.3 7.3 %all-to-all-start = ((f32[32,4,1024]{2,1,0:T(4,128)}), f32[32,4,1024]{2,1,0:T(4,128)S(1)}, u32[]{:S(2)}, u32[]{:S(2)}) async-start(f32[32,4,1024]{2,1,0:T(4,128)} %reshape.3148), calls=%async_computation | async-start | bytes 1048576 | tf_op jit(solution)/shard_map/all_to_all | solution.py:161
  106.8 45.2 %all-gather.1 = f32[32,2,2048]{2,1,0:T(2,128)S(1)} all-gather(f32[1,2,2048]{2,1,0:T(2,128)S(1)} %bitcast.502), channel_id=2, replica_groups=mesh['src'=8,'att'=4] {'src','att'}, dimensions={0}, use_global_device_ids=true | all-gather | bytes 540672 | tf_op jit(solution)/shard_map/all_gather | solution.py:162
  152.3 0.6 stack.118
  154.2 0.9 copy.46
  155.0 2.6 all-to-all-start.1
  158.3 9.9 %all-to-all-done.1 = f32[32,4,512]{2,1,0:T(4,128)S(1)} async-done(((f32[32,4,512]{2,1,0:T(4,128)}), f32[32,4,512]{2,1,0:T(4,128)S(1)}, u32[]{:S(2)}, u32[]{:S(2)}) %all-to-all-start.1) | async-done | bytes 262176 | tf_op jit(solution)/shard_map/all_to_all | solution.py:182
  168.3 90.2 %while.24 = (s32[]{:T(128)}, f32[4,2048]{1,0:T(4,128)S(1)}, f32[4,2048]{1,0:T(4,128)S(1)}, s32[4,2048]{1,0:T(4,128)S(1)}, f32[4,2048,4]{1,2,0:T(4,128)S(1)}, /*i...) while((s32[]{:T(128)}, f32[4,2048]{1,0:T(4,128)S(1)}, ...), condition=%wide.region_7.8_spmd.clone, body=%wide.region_4.7_spmd.clone.sunk | while | flops 1670653952 | bytes 19644568 | solution.py:212
  168.4 7.5 %fusion.130 = f32[1,2048]{1,0:T(1,128)S(1)} fusion(f32[2048,1]{0,1:T(1,128)S(1)} %bitcast.506, s32[2048]{0:T(1024)S(1)} %bitcast.472), kind=kOutput, calls=%fused_computation.5.clone.1 | convolution fusion | flops 54525952 | bytes 24576 | tf_op jit(solution)/shard_map/while/body/eval_jaxpr/dot_general | solution.py:198
  175.9 3.7 %fusion.131 = f32[2048,512]{0,1:T(8,128)} fusion(f32[128,512]{1,0:T(8,128)S(1)} %get-tuple-element.635, s32[2048]{0:T(1024)S(1)} %bitcast.447), kind=kOutput, calls=%fused_computation.14.clone.1 | convolution fusion | flops 1610874880 | bytes 4464640 | tf_op jit(solution)/shard_map/while/body/eval_jaxpr/dot_general | solution.py:190
  179.7 5.2 %reshape.3270 = f32[2048,128,4]{0,2,1:T(4,128)} reshape(f32[2048,512]{0,1:T(8,128)} %fusion.131) | data formatting | bytes 8388608 | tf_op jit(solution)/shard_map/while/body/eval_jaxpr/reshape | solution.py:193
  184.8 5.3 %multiply_reduce_fusion.5 = f32[2048,128]{0,1:T(8,128)S(1)} fusion(f32[2048,128,4]{0,2,1:T(4,128)} %reshape.3270, f32[2048,4]{0,1:T(4,128)S(1)} %get-tuple-element.531), kind=kLoop, calls=%fused_computation.7.clone.1 | loop fusion | flops 1835008 | bytes 5275648 | tf_op jit(solution)/shard_map/while/body/eval_jaxpr/reduce_sum | solution.py:194
  190.9 7.5 %fusion.130 = f32[1,2048]{1,0:T(1,128)S(1)} fusion(f32[2048,1]{0,1:T(1,128)S(1)} %bitcast.506, s32[2048]{0:T(1024)S(1)} %bitcast.472), kind=kOutput, calls=%fused_computation.5.clone.1 | convolution fusion | flops 54525952 | bytes 24576 | tf_op jit(solution)/shard_map/while/body/eval_jaxpr/dot_general | solution.py:198
  198.5 3.7 %fusion.131 = f32[2048,512]{0,1:T(8,128)} fusion(f32[128,512]{1,0:T(8,128)S(1)} %get-tuple-element.635, s32[2048]{0:T(1024)S(1)} %bitcast.447), kind=kOutput, calls=%fused_computation.14.clone.1 | convolution fusion | flops 1610874880 | bytes 4464640 | tf_op jit(solution)/shard_map/while/body/eval_jaxpr/dot_general | solution.py:190
  202.2 5.2 %reshape.3270 = f32[2048,128,4]{0,2,1:T(4,128)} reshape(f32[2048,512]{0,1:T(8,128)} %fusion.131) | data formatting | bytes 8388608 | tf_op jit(solution)/shard_map/while/body/eval_jaxpr/reshape | solution.py:193
  207.4 5.3 %multiply_reduce_fusion.5 = f32[2048,128]{0,1:T(8,128)S(1)} fusion(f32[2048,128,4]{0,2,1:T(4,128)} %reshape.3270, f32[2048,4]{0,1:T(4,128)S(1)} %get-tuple-element.531), kind=kLoop, calls=%fused_computation.7.clone.1 | loop fusion | flops 1835008 | bytes 5275648 | tf_op jit(solution)/shard_map/while/body/eval_jaxpr/reduce_sum | solution.py:194
  213.5 7.5 %fusion.130 = f32[1,2048]{1,0:T(1,128)S(1)} fusion(f32[2048,1]{0,1:T(1,128)S(1)} %bitcast.506, s32[2048]{0:T(1024)S(1)} %bitcast.472), kind=kOutput, calls=%fused_computation.5.clone.1 | convolution fusion | flops 54525952 | bytes 24576 | tf_op jit(solution)/shard_map/while/body/eval_jaxpr/dot_general | solution.py:198
  221.0 3.7 %fusion.131 = f32[2048,512]{0,1:T(8,128)} fusion(f32[128,512]{1,0:T(8,128)S(1)} %get-tuple-element.635, s32[2048]{0:T(1024)S(1)} %bitcast.447), kind=kOutput, calls=%fused_computation.14.clone.1 | convolution fusion | flops 1610874880 | bytes 4464640 | tf_op jit(solution)/shard_map/while/body/eval_jaxpr/dot_general | solution.py:190
  224.7 5.2 %reshape.3270 = f32[2048,128,4]{0,2,1:T(4,128)} reshape(f32[2048,512]{0,1:T(8,128)} %fusion.131) | data formatting | bytes 8388608 | tf_op jit(solution)/shard_map/while/body/eval_jaxpr/reshape | solution.py:193
  229.9 5.3 %multiply_reduce_fusion.5 = f32[2048,128]{0,1:T(8,128)S(1)} fusion(f32[2048,128,4]{0,2,1:T(4,128)} %reshape.3270, f32[2048,4]{0,1:T(4,128)S(1)} %get-tuple-element.531), kind=kLoop, calls=%fused_computation.7.clone.1 | loop fusion | flops 1835008 | bytes 5275648 | tf_op jit(solution)/shard_map/while/body/eval_jaxpr/reduce_sum | solution.py:194
  236.0 7.5 %fusion.130 = f32[1,2048]{1,0:T(1,128)S(1)} fusion(f32[2048,1]{0,1:T(1,128)S(1)} %bitcast.506, s32[2048]{0:T(1024)S(1)} %bitcast.472), kind=kOutput, calls=%fused_computation.5.clone.1 | convolution fusion | flops 54525952 | bytes 24576 | tf_op jit(solution)/shard_map/while/body/eval_jaxpr/dot_general | solution.py:198
  243.5 3.7 %fusion.131 = f32[2048,512]{0,1:T(8,128)} fusion(f32[128,512]{1,0:T(8,128)S(1)} %get-tuple-element.635, s32[2048]{0:T(1024)S(1)} %bitcast.447), kind=kOutput, calls=%fused_computation.14.clone.1 | convolution fusion | flops 1610874880 | bytes 4464640 | tf_op jit(solution)/shard_map/while/body/eval_jaxpr/dot_general | solution.py:190
  247.3 5.2 %reshape.3270 = f32[2048,128,4]{0,2,1:T(4,128)} reshape(f32[2048,512]{0,1:T(8,128)} %fusion.131) | data formatting | bytes 8388608 | tf_op jit(solution)/shard_map/while/body/eval_jaxpr/reshape | solution.py:193
  252.4 5.3 %multiply_reduce_fusion.5 = f32[2048,128]{0,1:T(8,128)S(1)} fusion(f32[2048,128,4]{0,2,1:T(4,128)} %reshape.3270, f32[2048,4]{0,1:T(4,128)S(1)} %get-tuple-element.531), kind=kLoop, calls=%fused_computation.7.clone.1 | loop fusion | flops 1835008 | bytes 5275648 | tf_op jit(solution)/shard_map/while/body/eval_jaxpr/reduce_sum | solution.py:194
  (155 shorter events, 11.8 us)
Async XLA Ops:
  0.6 0.7 copy-start
  0.6 10.0 %copy-start.1 = (f32[5,8192]{1,0:T(8,128)S(1)}, f32[5,8192]{1,0:T(8,128)}, u32[]{:S(2)}) copy-start(f32[5,8192]{1,0:T(8,128)} %param.19) | copy-start | bytes 491524
  0.7 10.1 %copy-start.3 = (f32[8192]{0:T(1024)S(1)}, f32[8192]{0:T(1024)}, u32[]{:S(2)}) copy-start(f32[8192]{0:T(1024)} %param.21) | copy-start | bytes 98308
  0.7 10.1 %copy-start.4 = (f32[8192]{0:T(1024)S(1)}, f32[8192]{0:T(1024)}, u32[]{:S(2)}) copy-start(f32[8192]{0:T(1024)} %param.17) | copy-start | bytes 98308
  0.7 7.3 %copy-start.5 = (s32[8192]{0:T(1024)S(1)}, s32[8192]{0:T(1024)}, u32[]{:S(2)}) copy-start(s32[8192]{0:T(1024)} %param.25) | copy-start | bytes 98308
  0.7 7.3 %copy-start.6 = (s32[8192]{0:T(1024)S(1)}, s32[8192]{0:T(1024)}, u32[]{:S(2)}) copy-start(s32[8192]{0:T(1024)} %param.24) | copy-start | bytes 98308
  0.7 7.4 %copy-start.8 = (s32[8192]{0:T(1024)S(1)}, s32[8192]{0:T(1024)}, u32[]{:S(2)}) copy-start(s32[8192]{0:T(1024)} %param.26) | copy-start | bytes 98308
  0.7 7.4 %copy-start.7 = (f32[8192]{0:T(1024)S(1)}, f32[8192]{0:T(1024)}, u32[]{:S(2)}) copy-start(f32[8192]{0:T(1024)} %param.22) | copy-start | bytes 98308
  0.7 10.1 %copy-start.9 = (s32[8192]{0:T(1024)S(1)}, s32[8192]{0:T(1024)}, u32[]{:S(2)}) copy-start(s32[8192]{0:T(1024)} %param.27) | copy-start | bytes 98308
  0.7 10.1 %copy-start.2 = (f32[4,8192]{1,0:T(4,128)S(1)}, f32[4,8192]{1,0:T(4,128)}, u32[]{:S(2)}) copy-start(f32[4,8192]{1,0:T(4,128)} %param.20) | copy-start | bytes 393220
  11.1 95.5 %copy-start.10 = (s32[32,1,4]{0,2,1:T(4,128)S(1)}, s32[32,1,4]{0,2,1:T(4,128)}, u32[]{:S(2)}) copy-start(s32[32,1,4]{0,2,1:T(4,128)} %param.29) | copy-start | bytes 1540
  99.3 53.6 %all-to-all-start = ((f32[32,4,1024]{2,1,0:T(4,128)}), f32[32,4,1024]{2,1,0:T(4,128)S(1)}, u32[]{:S(2)}, u32[]{:S(2)}) async-start(f32[32,4,1024]{2,1,0:T(4,128)} %reshape.3148), calls=%async_computation | async-start | bytes 1048576 | tf_op jit(solution)/shard_map/all_to_all | solution.py:161
  155.0 13.2 %all-to-all-start.1 = ((f32[32,4,512]{2,1,0:T(4,128)}), f32[32,4,512]{2,1,0:T(4,128)S(1)}, u32[]{:S(2)}, u32[]{:S(2)}) async-start(f32[32,4,512]{2,1,0:T(4,128)} %copy.46), calls=%async_computation.1 | async-start | bytes 524288 | tf_op jit(solution)/shard_map/all_to_all | solution.py:182
  258.5 0.6 copy-start.11
